TPU v7x, 128 devices: a whole 4x4x4 slice. The times are simulated.
128 devices in a mesh: grp: 8 (over y, core), seq: 16 (over x, z).
Axes of the slice: x: 4, y: 4, z: 4, core: 2. Of those that a mesh axis runs over, the one named last changes fastest.
Arguments:
- prefill_cache: bfloat16 [128, 16384, 576], P('grp', 'seq'), may hold values from -9 to 9
- lengths: int32 [128], replicated, may hold values from 2 to 16384, as said below
- decode_slots: int32 [8, 16], replicated, may hold values from 0 to 127, as said below
- q_nope: bfloat16 [2, 128, 16384], P(None, 'grp', 'seq'), may hold values from -6 to 6
- q_pe: bfloat16 [2, 128, 8192], P(None, 'grp', 'seq'), may hold values from -8 to 8
- new_latent: bfloat16 [2, 128, 576], P(None, 'grp'), may hold values from -6 to 6
- w_uk: bfloat16 [128, 128, 512], P('seq'), may hold values from -0.5 to 0.5
- value_up_weight: bfloat16 [128, 512, 128], P('seq'), may hold values from -0.25 to 0.25
Outputs:
- attended: bfloat16 [2, 128, 16384], P(None, 'grp', 'seq')
Inputs may be any that keep to these rules, and one draw needn't show every extreme that they name: `decode_slots`: every request id appears exactly once. Of the 16 requests of one row, at most 3 lie in one aligned run of 16 request ids; every run has 3 requests in some row. `lengths`: some request has exactly 16384 rows.
All inputs are finite; a program needn't handle non-finite values.
Results may differ from a plain program's by a relative error of at most 0.018.
Values may be sent and summed in bfloat16 or wider, within the bound.
A program may use at most 192 MiB of HBM per device.

v0:
```python
import functools

import jax
import jax.numpy as jnp
from jax import lax
from jax.experimental import pallas as pl
from jax.experimental.pallas import tpu as pltpu
from jax.sharding import PartitionSpec as P

MESH = pl.DeviceIdType.MESH
LOG2E = 1.4426950408889634
LOW = -1e30
CAP = 3
NX = 4
NZ = 4
F32 = jnp.float32
BF16 = jnp.bfloat16


def dot(a, b):
    return jnp.dot(a, b, preferred_element_type=F32)


def dot_nt(a, b):
    return lax.dot_general(a, b, (((1,), (1,)), ((), ())), preferred_element_type=F32)


def iota(shape, dim):
    return lax.broadcasted_iota(jnp.int32, shape, dim)


def pick(cond):
    return jnp.where(cond, 1.0, 0.0).astype(BF16)


def kernel(
    ngrp, nreq, blk, scale2,
    lens, slots, qn, qp, lat, w_uk_hbm, w_v_hbm, cache,
    out,
    cbuf, w_uk, w_v, tx, rx, latrep, qall, pout, lrow, h1, lh1, r1, lr1, red1, lred, r2, lr2,
    fin, flse, tx2, rx2,
    c_sem, w_sem, out_sem, rt_r, rb_r, g1_r, g2_r, g3_r, h_r, s1_r, s2_r,
):
    g = lax.axis_index("grp")
    s = lax.axis_index("seq")
    x = lax.div(s, NZ)
    z = lax.rem(s, NZ)
    half = nreq // 2
    rows = nreq * 16
    lw = 512
    c_copies = [pltpu.make_async_copy(cache.at[r], cbuf.at[r], c_sem.at[r]) for r in range(nreq)]
    w_copies = [
        pltpu.make_async_copy(w_uk_hbm, w_uk, w_sem.at[0]),
        pltpu.make_async_copy(w_v_hbm, w_v, w_sem.at[1]),
    ]
    for c in w_copies + c_copies:
        c.start()

    def gid(k):
        return {"grp": lax.rem(g + k, ngrp)}

    def xid(k):
        return {"seq": lax.rem(x + k, NX) * NZ + z}

    def zid(k):
        return {"seq": x * NZ + lax.rem(z + k, NZ)}

    def rcopy(src, dst, ss, rs, dev):
        return pltpu.make_async_remote_copy(
            src_ref=src, dst_ref=dst, send_sem=ss, recv_sem=rs, device_id=dev, device_id_type=MESH
        )

    barrier = pltpu.get_barrier_semaphore()
    for k in range(1, ngrp):
        pl.semaphore_signal(barrier, inc=1, device_id=gid(k), device_id_type=MESH)
    for k in range(1, 4):
        pl.semaphore_signal(barrier, inc=1, device_id=xid(k), device_id_type=MESH)
        pl.semaphore_signal(barrier, inc=1, device_id=zid(k), device_id_type=MESH)

    shift = nreq.bit_length() - 1
    served = slots[...]
    dest = lax.shift_right_logical(served, shift)
    lane_s = iota((ngrp, nreq), 1)
    rank = jnp.zeros((ngrp, nreq), jnp.int32)
    for j in range(nreq - 1):
        rank += jnp.where((dest == dest[:, j : j + 1]) & (lane_s > j), 1, 0)
    origin = iota((ngrp, nreq), 0) * 16 + 2 * rank
    mine = iota((ngrp, nreq), 0) == g
    rho = jnp.sum(jnp.where(mine, dest * 16 + 2 * rank, 0), axis=0, keepdims=True)
    row_id = iota((rows, nreq), 0)
    asked = g * nreq + row_id // 16
    sig = jnp.zeros((rows, nreq), jnp.int32)
    for j in range(ngrp):
        sig += jnp.where(served[j : j + 1, :] == asked, origin[j : j + 1, :], 0)
    sig = jnp.sum(sig, axis=1, keepdims=True) + (iota((rows, 1), 0) // 8) % 2

    bl = ngrp * 16
    row_l = iota((bl, nreq), 0)
    sends = [[jnp.where(row_l == rho + t + 2 * CAP * f, 1.0, 0.0) for t in range(2)] for f in range(2)]

    def send_dot(f, cols):
        both = [dot(sends[f][t].astype(BF16), cols(pl.ds(t * nreq, nreq))) for t in range(2)]
        return both[0] + both[1]

    head = send_dot(0, lambda r: qn[r, :lw]) + send_dot(1, lambda r: qp[r, :])
    tx[:, :, :lw] = head.astype(BF16).reshape(ngrp, 16, lw)
    mid = send_dot(0, lambda r: qn[r, lw:]) + send_dot(1, lambda r: lat[r, :lw])
    tx[:, :, lw : 2 * lw] = mid.astype(BF16).reshape(ngrp, 16, lw)
    tail = send_dot(1, lambda r: lat[r, lw:])
    tx[:, :, 2 * lw :] = tail.astype(BF16).reshape(ngrp, 16, 64)

    pl.semaphore_wait(barrier, ngrp - 1 + 6)
    route = [
        rcopy(tx.at[lax.rem(g + k, ngrp)], rx.at[g], out_sem.at[9], rt_r.at[0], gid(k))
        for k in range(1, ngrp)
    ]
    for c in route:
        c.start()
    rx[g] = tx[g]
    most = pl.ds(0, ngrp - 1)
    all_routed = rcopy(tx.at[most], rx.at[most], out_sem.at[9], rt_r.at[0], gid(1))
    all_routed.wait_recv()

    col_l = iota((rows, bl), 1)
    pulls = [jnp.where(col_l == sig + 2 * CAP * f, 1.0, 0.0) for f in range(2)]
    m0, m1 = [v.astype(BF16) for v in pulls]
    own = iota((rows, lw), 0) % 8
    lane = iota((rows, lw), 1)
    w_copies[0].wait()
    absorbed = jnp.zeros((rows, lw), F32)
    for j in range(2):
        spread = dot(m0, rx[:, :, j * lw : (j + 1) * lw].reshape(bl, lw))
        spread = jnp.where(lane // 128 + 4 * j == own, spread, 0.0).astype(BF16)
        absorbed += dot(spread, w_uk[j * lw : (j + 1) * lw, :])
    qall[:, x, z, :, :lw] = absorbed.astype(BF16).reshape(nreq, 16, lw)
    spread = dot(m1, rx[:, :, :lw].reshape(bl, lw))
    spread = jnp.where(lane // 64 == own, spread, 0.0).astype(BF16)
    fold = pick(iota((lw, 64), 0) % 64 == iota((lw, 64), 1))
    qall[:, x, z, :, lw:] = dot(spread, fold).astype(BF16).reshape(nreq, 16, 64)

    xl = lax.rem(x + 3, NX)
    xr = lax.rem(x + 1, NX)
    xo = lax.rem(x + 2, NX)
    zl = lax.rem(z + 3, NZ)
    zr = lax.rem(z + 1, NZ)
    zo = lax.rem(z + 2, NZ)
    two = (pl.ds(0, 2), pl.ds(2, 2))

    def start(copies):
        for c in copies:
            c.start()

    def landed(ref, sem):
        rcopy(ref, ref, out_sem.at[0], sem, xid(1)).wait_recv()

    def near(i):
        copies = []
        for k in (1, 3, 2):
            a, b = qall.at[i, x, z], qall.at[half + i, x, z]
            copies.append(rcopy(a, a, out_sem.at[0], g1_r.at[i], zid(k)))
            copies.append(rcopy(b, b, out_sem.at[0], g1_r.at[i], xid(k)))
        return copies

    def near_in(i):
        landed(qall.at[i, pl.ds(0, 2), pl.ds(0, 3)], g1_r.at[i])

    def direct(i):
        a = qall.at[i, x]
        b = qall.at[half + i, :, z]
        return [
            rcopy(ref, ref, out_sem.at[1], g2_r.at[i], dev)
            for ref, dev in ((a, xid(1)), (b, zid(1)), (a, xid(3)), (b, zid(3)))
        ]

    def direct_in(i):
        landed(qall.at[i], g2_r.at[i])

    def onward(i):
        moves = (
            (qall.at[i, xl, two[0]], xid(1)), (qall.at[half + i, two[0], zl], zid(1)),
            (qall.at[i, xr, two[1]], xid(3)), (qall.at[half + i, two[1], zr], zid(3)),
        )
        return [rcopy(ref, ref, out_sem.at[2], g3_r.at[i], dev) for ref, dev in moves]

    def onward_in(i):
        landed(qall.at[i, pl.ds(0, 2)], g3_r.at[i])

    def relay(i):
        direct_in(i)
        start(onward(i))

    first = 2
    for i in range(first):
        start(near(i))

    latrep[:, :lw] = dot(m1, rx[:, :, lw : 2 * lw].reshape(bl, lw)).astype(BF16)
    latrep[:, lw:] = dot(m1, rx[:, :, 2 * lw :].reshape(bl, 64)).astype(BF16)
    qo = qall[:, x, z].reshape(rows, lw + 64)
    fresh = dot_nt(qo[:, :lw], latrep[:, :lw]) + dot_nt(qo[:, lw:], latrep[:, lw:])
    ri = iota((rows, rows), 0)
    ci = iota((rows, rows), 1)
    seen = (ri // 16 == ci // 16) & ((ci // 8) % 2 <= (ri // 8) % 2) & (ci % 8 == 0)
    fresh = jnp.where(seen, fresh * scale2, LOW)
    ftop = jnp.max(fresh, axis=1, keepdims=True)
    wf = jnp.where(seen, jnp.exp2(fresh - ftop), 0.0)
    fden = jnp.sum(wf, axis=1, keepdims=True)
    fnum = dot(wf.astype(BF16), latrep[:, :lw])

    def send(src, dst, ls, ld, n, rs, i, dev):
        return [
            rcopy(src, dst, out_sem.at[n], rs.at[0, i], dev),
            rcopy(ls, ld, out_sem.at[n + 1], rs.at[1, i], dev),
        ]

    def far(i):
        copies = []
        for j in range(2):
            a, b = pout.at[i, xo, two[j]], pout.at[half + i, two[j], zo]
            copies += send(a, h1.at[0, j, i], lrow.at[i, xo], lh1.at[0, j, i], 3, h_r, i,
                           xid(1 + 2 * j))
            copies += send(b, h1.at[1, j, i], lrow.at[half + i, zo], lh1.at[1, j, i], 3, h_r, i,
                           zid(1 + 2 * j))
        return copies

    def far_in(i):
        landed(pout.at[i, pl.ds(0, 2)], h_r.at[0, i])
        landed(lrow.at[i], h_r.at[1, i])

    def scatter1(i):
        copies = []
        for j in range(2):
            xt, zt = (xr, xl)[j], (zr, zl)[j]
            copies += send(pout.at[i, xt], r1.at[0, j, i], lrow.at[i, xt], lr1.at[0, j, i],
                           5, s1_r, i, xid(1 + 2 * j))
            copies += send(pout.at[half + i, :, zt], r1.at[1, j, i], lrow.at[half + i, zt],
                           lr1.at[1, j, i], 5, s1_r, i, zid(1 + 2 * j))
        return copies

    def scatter1_in(i):
        landed(pout.at[i], s1_r.at[0, i])
        landed(lrow.at[i], s1_r.at[1, i])

    def scatter2(i):
        copies = []
        for k in (1, 3, 2):
            copies += send(red1.at[0, i, lax.rem(z + k, NZ)], r2.at[0, k - 1, i], lred.at[0, i],
                           lr2.at[0, k - 1, i], 7, s2_r, i, zid(k))
            copies += send(red1.at[1, i, lax.rem(x + k, NX)], r2.at[1, k - 1, i], lred.at[1, i],
                           lr2.at[1, k - 1, i], 7, s2_r, i, xid(k))
        return copies

    def scatter2_in(i):
        landed(pout.at[i, pl.ds(0, 2), pl.ds(0, 3)], s2_r.at[0, i])
        landed(lrow.at[pl.ds(0, 2), pl.ds(0, 3)], s2_r.at[1, i])

    def weights(ls):
        top = functools.reduce(jnp.maximum, ls)
        ws = [jnp.exp2(v - top) for v in ls]
        total = functools.reduce(jnp.add, ws)
        inv = 1.0 / total
        return [w * inv for w in ws], top + jnp.log2(total)

    def column(w, n, off):
        shape = (n, 128)
        return jnp.sum(
            jnp.where(iota(shape, 1) == iota(shape, 0) + off, w, 0.0), axis=1, keepdims=True
        )

    def blend(blocks, ws, n, off):
        acc = 0.0
        for b, w in zip(blocks, ws):
            acc += column(w, n, off) * b.reshape(n, lw).astype(F32)
        return acc

    nq = 16 * NX * NZ
    row_q = iota((nq, 128), 0)
    lane_q = iota((nq, 128), 1)

    def attend(r, part):
        pltpu.make_async_copy(cache.at[r], cbuf.at[r], c_sem.at[r]).wait()
        q = qall[r].reshape(nq, lw + 64)
        c = cbuf.at[r]
        sc = dot(q[:, :lw], c[:lw, :]) + dot(q[:, lw:], c[lw:, :])
        place = s * blk + iota((1, blk), 1)
        sc = sc + jnp.where(place < lens[g * nreq + r], 0.0, LOW)
        top = jnp.max(sc, axis=1, keepdims=True)
        w = jnp.exp2((sc - top) * scale2)
        den = jnp.sum(w, axis=1, keepdims=True)
        num = dot_nt(w.astype(BF16), c[:lw, :])
        pout[r] = (num * (1.0 / den)).astype(BF16).reshape(NX, NZ, 16, lw)
        lse = top * scale2 + jnp.log2(den)
        if part == 0:
            diag = jnp.where(lane_q == row_q % 64, lse, 0.0).reshape(4, 64, 128)
        else:
            diag = jnp.where(lane_q == row_q // 64 * 16 + row_q % 16, lse, 0.0)
            diag = jnp.sum(diag.reshape(4, 4, 16, 128), axis=0)
        for d in range(4):
            lrow[r, d] = jnp.sum(diag[d], axis=0, keepdims=True)

    lane_1 = iota((1, 128), 1)

    def middle(i):
        for j in range(2):
            xt, zt = (xr, xl)[j], (zr, zl)[j]
            keep = (lane_1 < 32) if j == 0 else (lane_1 >= 32)
            ws, ln = weights([lrow[i, xt], lh1[0, j, i]])
            acc = blend([pout[i, xt, two[j]], h1[0, j, i]], ws, 32, 32 * j)
            pout[i, xt, two[j]] = acc.astype(BF16).reshape(2, 16, lw)
            lrow[i, xt] = jnp.where(keep, ln, lrow[i, xt])
            r = half + i
            ws, ln = weights([lrow[r, zt], lh1[1, j, i]])
            acc = blend([pout[r, two[j], zt], h1[1, j, i]], ws, 32, 32 * j)
            pout[r, two[j], zt] = acc.astype(BF16).reshape(2, 16, lw)
            lrow[r, zt] = jnp.where(keep, ln, lrow[r, zt])

    def reduce1(i):
        ws, ln = weights([lrow[i, x], lr1[0, 0, i], lr1[0, 1, i]])
        acc = blend([pout[i, x], r1[0, 0, i], r1[0, 1, i]], ws, 64, 0)
        red1[0, i] = acc.astype(BF16).reshape(4, 16, lw)
        lred[0, i] = ln
        ws, ln = weights([lrow[half + i, z], lr1[1, 0, i], lr1[1, 1, i]])
        acc = blend([pout[half + i, :, z], r1[1, 0, i], r1[1, 1, i]], ws, 64, 0)
        red1[1, i] = acc.astype(BF16).reshape(4, 16, lw)
        lred[1, i] = ln

    def reduce2(i):
        for part, own in ((0, z), (1, x)):
            ws, ln = weights([lred[part, i]] + [lr2[part, k, i] for k in range(3)])
            blocks = [red1[part, i, own]] + [r2[part, k, i] for k in range(3)]
            fin[part * half + i] = blend(blocks, ws, 16, own * 16)
            flse[part * half + i] = jnp.broadcast_to(column(ln, 16, own * 16), (16, 128))

    def step(t, carry):
        @pl.when(t + first < half)
        def _():
            start(near(t + first))

        @pl.when(t < half)
        def _():
            near_in(t)
            start(direct(t))

        i1 = t - 1

        @pl.when((i1 >= 0) & (i1 < half))
        def _():
            relay(i1)

        i2 = t - 2

        @pl.when((i2 >= 0) & (i2 < half))
        def _():
            onward_in(i2)
            attend(i2, 0)
            attend(half + i2, 1)
            start(far(i2))

        i3 = t - 3

        @pl.when((i3 >= 0) & (i3 < half))
        def _():
            far_in(i3)
            middle(i3)
            start(scatter1(i3))

        i5 = t - 5

        @pl.when((i5 >= 0) & (i5 < half))
        def _():
            scatter1_in(i5)
            reduce1(i5)
            start(scatter2(i5))

        i7 = t - 7

        @pl.when(i7 >= 0)
        def _():
            scatter2_in(i7)
            reduce2(i7)

        return carry

    lax.fori_loop(0, half + 7, step, 0)

    w_copies[1].wait()
    lse = flse[...].reshape(rows, 128)[:, :1]
    top = jnp.maximum(ftop, lse)
    wc = jnp.exp2(lse - top)
    wn = jnp.exp2(ftop - top)
    den = wc + wn * fden
    num = wc * fin[...].reshape(rows, lw) + wn * fnum
    latent = (num * (1.0 / den)).astype(BF16)
    b0, b1 = [v.T.astype(BF16) for v in pulls]
    hrow = iota((rows, 128), 0) % 8
    for j in range(4):
        va0 = jnp.where(hrow == j, dot(latent, w_v[j]), 0.0).astype(BF16)
        vb0 = jnp.where(hrow == j + 4, dot(latent, w_v[j + 4]), 0.0).astype(BF16)
        back = dot(b0, va0) + dot(b1, vb0)
        tx2[:, :, j * 128 : (j + 1) * 128] = back.astype(BF16).reshape(ngrp, 16, 128)

    home = [
        rcopy(tx2.at[lax.rem(g + k, ngrp)], rx2.at[g], out_sem.at[10], rb_r.at[0], gid(k))
        for k in range(1, ngrp)
    ]
    start(home)
    rx2[g] = tx2[g]

    def left(ref, n):
        rcopy(ref, ref, out_sem.at[n], s1_r.at[0, 0], xid(1)).wait_send()

    left(qall.at[pl.ds(0, 3)], 0)
    left(qall.at[pl.ds(0, 8)], 1)
    left(qall.at[pl.ds(0, 4)], 2)
    left(pout.at[pl.ds(0, 4)], 3)
    left(lrow.at[pl.ds(0, 8)], 4)
    left(pout.at[pl.ds(0, 8)], 5)
    left(lrow.at[pl.ds(0, 8)], 6)
    left(pout.at[pl.ds(0, 3)], 7)
    left(lrow.at[pl.ds(0, 12)], 8)
    all_routed.wait_send()
    all_home = rcopy(tx2.at[most], rx2.at[most], out_sem.at[10], rb_r.at[0], gid(1))
    all_home.wait_recv()
    got = rx2[...].reshape(bl, lw)
    for f in range(2):
        for t in range(2):
            kept = dot(sends[f][t].T.astype(BF16), got)
            out[pl.ds(t * nreq, nreq), pl.ds(f * lw, lw)] = kept.astype(BF16)

    all_home.wait_send()


def on_device(
    prefill_cache, lengths, decode_slots, q_nope, q_pe, new_latent, w_uk, value_up_weight
):
    ngrp = lax.axis_size("grp")
    nreq, blk, width = prefill_cache.shape
    steps = new_latent.shape[0]
    heads, nope, lw = w_uk.shape
    half = nreq // 2
    scale2 = (nope + width - lw) ** -0.5 * LOG2E

    rows = nreq * steps * heads
    vm = pl.BlockSpec(memory_space=pltpu.VMEM)
    dma = pltpu.SemaphoreType.DMA
    bytes_in = 2 * prefill_cache.size
    out = pl.pallas_call(
        functools.partial(kernel, ngrp, nreq, blk, scale2),
        out_shape=jax.ShapeDtypeStruct((steps * nreq, heads * 128), BF16),
        in_specs=[pl.BlockSpec(memory_space=pltpu.SMEM)] + [vm] * 4
        + [pl.BlockSpec(memory_space=pl.ANY)] * 3,
        out_specs=vm,
        scratch_shapes=[
            pltpu.VMEM((nreq, width, blk), BF16),
            pltpu.VMEM((heads * nope, lw), BF16),
            pltpu.VMEM((heads, lw, 128), BF16),
            pltpu.VMEM((ngrp, 16, 1088), BF16),
            pltpu.VMEM((ngrp, 16, 1088), BF16),
            pltpu.VMEM((rows, width), BF16),
            pltpu.VMEM((nreq, NX, NZ, 16, width), BF16),
            pltpu.VMEM((nreq, NX, NZ, 16, lw), BF16),
            pltpu.VMEM((nreq, 4, 1, 128), F32),
            pltpu.VMEM((2, 2, half, 2, 16, lw), BF16),
            pltpu.VMEM((2, 2, half, 1, 128), F32),
            pltpu.VMEM((2, 2, half, 4, 16, lw), BF16),
            pltpu.VMEM((2, 2, half, 1, 128), F32),
            pltpu.VMEM((2, half, 4, 16, lw), BF16),
            pltpu.VMEM((2, half, 1, 128), F32),
            pltpu.VMEM((2, 3, half, 16, lw), BF16),
            pltpu.VMEM((2, 3, half, 1, 128), F32),
            pltpu.VMEM((nreq, 16, lw), F32),
            pltpu.VMEM((nreq, 16, 128), F32),
            pltpu.VMEM((ngrp, 16, lw), BF16),
            pltpu.VMEM((ngrp, 16, lw), BF16),
            dma((nreq,)), dma((2,)), dma((11,)), dma((1,)), dma((1,)),
            dma((half,)), dma((half,)), dma((half,)),
            dma((2, half)), dma((2, half)), dma((2, half)),
        ],
        compiler_params=pltpu.CompilerParams(
            collective_id=0, has_side_effects=True, vmem_limit_bytes=58 * 1024 * 1024
        ),
        cost_estimate=pl.CostEstimate(
            flops=2 * nreq * 256 * blk * (width + lw), bytes_accessed=bytes_in,
            transcendentals=nreq * 256 * blk,
        ),
    )(
        lengths, decode_slots,
        q_nope.reshape(steps * nreq, -1), q_pe.reshape(steps * nreq, -1),
        new_latent.reshape(steps * nreq, -1), w_uk.reshape(heads * nope, lw),
        value_up_weight, jnp.swapaxes(prefill_cache, 1, 2),
    )
    return out.reshape(steps, nreq, -1)


def solution(mesh):
    return jax.shard_map(
        on_device,
        mesh=mesh,
        in_specs=(
            P("grp", "seq", None),
            P(),
            P(),
            P(None, "grp", "seq"),
            P(None, "grp", "seq"),
            P(None, "grp", None),
            P("seq", None, None),
            P("seq", None, None),
        ),
        out_specs=P(None, "grp", "seq"),
        check_vma=False,
    )
```

profile of v0, /device:TPU:1, one launch (start us, length us, event | category | flops | bytes accessed | tf_op | source)
XLA Modules:
  0.0 85.5 jit_solution(3218141229190576646)
XLA Ops:
  0.0 84.0 %shard_map.82 = bf16[32,1024]{1,0:T(8,128)(2,1)} custom-call(s32[128]{0:T(128)} %lens.1, s32[8,16]{1,0:T(8,128)} %slots.1, bf16[32,1024]{1,0:T(8,128)(2,1)} %bitcast.9, bf16[32,512]{1,0:T(8,128)(2,1)} %bitcast.11, bf16[32,576]{1,0:T(8,128)(2,1)} %bitcast.10, bf16[1024,512]{1,0:T(8,128)(2,1)} %bitcast.8, bf16[8,512,128]{2,1,0:T(8,128)(2,1)} %w_v_hbm.1, ...), custom_call_target="tpu_custom_call" | custom-call | flops 9126805504 | bytes 18874368 | tf_op jit(solution)/shard_map/pallas_call | solution.py:446
  84.0 1.5 %copy.10 = bf16[2,16,1024]{2,1,0:T(8,128)(2,1)} copy(bf16[2,16,1024]{2,1,0:T(8,128)(2,1)} %bitcast.6) | data formatting | bytes 131072
where the time goes:
time: 85.7 us; the launch traced here: 85.5 us
  Pallas kernels  84 us (98%)
  local copies, waits for them, and re-layouts  1.47 us (2%)
    pallas_call x1, Pallas kernels, on_device(): pl.pallas_call(functools.partial(kernel, ngrp, nreq, blk, scale2), out_sh...  84 us

commit v1 on v0

--- a/solution.py
+++ b/solution.py
@@ -37,9 +37,9 @@
     ngrp, nreq, blk, scale2,
     lens, slots, qn, qp, lat, w_uk_hbm, w_v_hbm, cache,
     out,
-    cbuf, w_uk, w_v, tx, rx, latrep, qall, pout, lrow, h1, lh1, r1, lr1, red1, lred, r2, lr2,
+    cbuf, w_uk, w_v, tx, rx, ty, ry, latrep, qall, qpe, pout, lrow, h1, lh1, r1, lr1, rd, lrd, red1, lred, r2, lr2,
     fin, flse, tx2, rx2,
-    c_sem, w_sem, out_sem, rt_r, rb_r, g1_r, g2_r, g3_r, h_r, s1_r, s2_r,
+    c_sem, w_sem, out_sem, rt_r, ru_r, rb_r, g1_r, g2_r, g3_r, e1_r, e2_r, e3_r, h_r, s1_r, s2_r,
 ):
     g = lax.axis_index("grp")
     s = lax.axis_index("seq")
@@ -102,23 +102,26 @@
         both = [dot(sends[f][t].astype(BF16), cols(pl.ds(t * nreq, nreq))) for t in range(2)]
         return both[0] + both[1]
 
-    head = send_dot(0, lambda r: qn[r, :lw]) + send_dot(1, lambda r: qp[r, :])
-    tx[:, :, :lw] = head.astype(BF16).reshape(ngrp, 16, lw)
-    mid = send_dot(0, lambda r: qn[r, lw:]) + send_dot(1, lambda r: lat[r, :lw])
-    tx[:, :, lw : 2 * lw] = mid.astype(BF16).reshape(ngrp, 16, lw)
+    head = send_dot(0, lambda r: qn[r, :lw]) + send_dot(1, lambda r: qn[r, lw:])
+    tx[...] = head.astype(BF16).reshape(ngrp, 16, lw)
+    mid = send_dot(0, lambda r: qp[r, :]) + send_dot(1, lambda r: lat[r, :lw])
+    ty[:, :, :lw] = mid.astype(BF16).reshape(ngrp, 16, lw)
     tail = send_dot(1, lambda r: lat[r, lw:])
-    tx[:, :, 2 * lw :] = tail.astype(BF16).reshape(ngrp, 16, 64)
-
+    ty[:, :, lw:] = tail.astype(BF16).reshape(ngrp, 16, 64)
     pl.semaphore_wait(barrier, ngrp - 1 + 6)
+    dst = [lax.rem(g + k, ngrp) for k in range(1, ngrp)]
     route = [
-        rcopy(tx.at[lax.rem(g + k, ngrp)], rx.at[g], out_sem.at[9], rt_r.at[0], gid(k))
-        for k in range(1, ngrp)
+        rcopy(tx.at[d], rx.at[g], out_sem.at[9], rt_r.at[0], {"grp": d}) for d in dst
+    ] + [
+        rcopy(ty.at[d], ry.at[g], out_sem.at[14], ru_r.at[0], {"grp": d}) for d in dst
     ]
     for c in route:
         c.start()
     rx[g] = tx[g]
+    ry[g] = ty[g]
     most = pl.ds(0, ngrp - 1)
     all_routed = rcopy(tx.at[most], rx.at[most], out_sem.at[9], rt_r.at[0], gid(1))
+    more_routed = rcopy(ty.at[most], ry.at[most], out_sem.at[14], ru_r.at[0], gid(1))
     all_routed.wait_recv()
 
     col_l = iota((rows, bl), 1)
@@ -129,15 +132,10 @@
     w_copies[0].wait()
     absorbed = jnp.zeros((rows, lw), F32)
     for j in range(2):
-        spread = dot(m0, rx[:, :, j * lw : (j + 1) * lw].reshape(bl, lw))
+        spread = dot((m0, m1)[j], rx[...].reshape(bl, lw))
         spread = jnp.where(lane // 128 + 4 * j == own, spread, 0.0).astype(BF16)
         absorbed += dot(spread, w_uk[j * lw : (j + 1) * lw, :])
-    qall[:, x, z, :, :lw] = absorbed.astype(BF16).reshape(nreq, 16, lw)
-    spread = dot(m1, rx[:, :, :lw].reshape(bl, lw))
-    spread = jnp.where(lane // 64 == own, spread, 0.0).astype(BF16)
-    fold = pick(iota((lw, 64), 0) % 64 == iota((lw, 64), 1))
-    qall[:, x, z, :, lw:] = dot(spread, fold).astype(BF16).reshape(nreq, 16, 64)
-
+    qall[:, x, z] = absorbed.astype(BF16).reshape(nreq, 16, lw)
     xl = lax.rem(x + 3, NX)
     xr = lax.rem(x + 1, NX)
     xo = lax.rem(x + 2, NX)
@@ -189,14 +187,58 @@
         direct_in(i)
         start(onward(i))
 
-    first = 2
+    quarter = half // 2
+
+    def near_pe(i):
+        copies = []
+        for k in (1, 3, 2):
+            a, b = qpe.at[i, x, z], qpe.at[quarter + i, x, z]
+            copies.append(rcopy(a, a, out_sem.at[11], e1_r.at[i], zid(k)))
+            copies.append(rcopy(b, b, out_sem.at[11], e1_r.at[i], xid(k)))
+        return copies
+
+    def near_pe_in(i):
+        landed(qpe.at[i, pl.ds(0, 2), pl.ds(0, 3)], e1_r.at[i])
+
+    def direct_pe(i):
+        a = qpe.at[i, x]
+        b = qpe.at[quarter + i, :, z]
+        return [
+            rcopy(ref, ref, out_sem.at[12], e2_r.at[i], dev)
+            for ref, dev in ((a, xid(1)), (b, zid(1)), (a, xid(3)), (b, zid(3)))
+        ]
+
+    def relay_pe(i):
+        landed(qpe.at[i], e2_r.at[i])
+        moves = (
+            (qpe.at[i, xl, two[0]], xid(1)), (qpe.at[quarter + i, two[0], zl], zid(1)),
+            (qpe.at[i, xr, two[1]], xid(3)), (qpe.at[quarter + i, two[1], zr], zid(3)),
+        )
+        start([rcopy(ref, ref, out_sem.at[13], e3_r.at[i], dev) for ref, dev in moves])
+
+    def onward_pe_in(i):
+        landed(qpe.at[i, pl.ds(0, 2)], e3_r.at[i])
+
+    first = 4
     for i in range(first):
         start(near(i))
 
-    latrep[:, :lw] = dot(m1, rx[:, :, lw : 2 * lw].reshape(bl, lw)).astype(BF16)
-    latrep[:, lw:] = dot(m1, rx[:, :, 2 * lw :].reshape(bl, 64)).astype(BF16)
-    qo = qall[:, x, z].reshape(rows, lw + 64)
-    fresh = dot_nt(qo[:, :lw], latrep[:, :lw]) + dot_nt(qo[:, lw:], latrep[:, lw:])
+    more_routed.wait_recv()
+    spread = dot(m0, ry[:, :, :lw].reshape(bl, lw))
+    spread = jnp.where(lane // 64 == own, spread, 0.0).astype(BF16)
+    fold = pick(iota((lw, 128), 0) % 64 == iota((lw, 128), 1) % 64)
+    twice = dot(spread, fold)
+    pairs = twice.reshape(half, 2, 16, 128)
+    side = iota((half, 16, 128), 2) < 64
+    qpe[:, x, z] = jnp.where(side, pairs[:, 0], pairs[:, 1]).astype(BF16)
+    own_pe = twice[:, :64].astype(BF16)
+    for i in range(0, first, 2):
+        start(near_pe(i // 2))
+
+    latrep[:, :lw] = dot(m1, ry[:, :, :lw].reshape(bl, lw)).astype(BF16)
+    latrep[:, lw:] = dot(m1, ry[:, :, lw:].reshape(bl, 64)).astype(BF16)
+    qo = qall[:, x, z].reshape(rows, lw)
+    fresh = dot_nt(qo, latrep[:, :lw]) + dot_nt(own_pe, latrep[:, lw:])
     ri = iota((rows, rows), 0)
     ci = iota((rows, rows), 1)
     seen = (ri // 16 == ci // 16) & ((ci // 8) % 2 <= (ri // 8) % 2) & (ci % 8 == 0)
@@ -226,6 +268,17 @@
         landed(pout.at[i, pl.ds(0, 2)], h_r.at[0, i])
         landed(lrow.at[i], h_r.at[1, i])
 
+    last = half - 1
+
+    def straight():
+        a, b = pout.at[last, xo], pout.at[half + last, :, zo]
+        return send(a, rd.at[0], lrow.at[last, xo], lrd.at[0], 3, h_r, last, xid(2)) + send(
+            b, rd.at[1], lrow.at[half + last, zo], lrd.at[1], 3, h_r, last, zid(2))
+
+    def straight_in():
+        landed(rd, h_r.at[0, last])
+        landed(lrd, h_r.at[1, last])
+
     def scatter1(i):
         copies = []
         for j in range(2):
@@ -278,9 +331,12 @@
 
     def attend(r, part):
         pltpu.make_async_copy(cache.at[r], cbuf.at[r], c_sem.at[r]).wait()
-        q = qall[r].reshape(nq, lw + 64)
+        q = qall[r].reshape(nq, lw)
+        pair = qpe[r // 2].reshape(nq, 128)
+        odd = jnp.full((1, 64), r % 2, F32).astype(BF16)
+        pe = pair[:, :64] * (1.0 - odd) + pair[:, 64:] * odd
         c = cbuf.at[r]
-        sc = dot(q[:, :lw], c[:lw, :]) + dot(q[:, lw:], c[lw:, :])
+        sc = dot(q, c[:lw, :]) + dot(pe, c[lw:, :])
         place = s * blk + iota((1, blk), 1)
         sc = sc + jnp.where(place < lens[g * nreq + r], 0.0, LOW)
         top = jnp.max(sc, axis=1, keepdims=True)
@@ -313,14 +369,17 @@
             pout[r, two[j], zt] = acc.astype(BF16).reshape(2, 16, lw)
             lrow[r, zt] = jnp.where(keep, ln, lrow[r, zt])
 
-    def reduce1(i):
-        ws, ln = weights([lrow[i, x], lr1[0, 0, i], lr1[0, 1, i]])
-        acc = blend([pout[i, x], r1[0, 0, i], r1[0, 1, i]], ws, 64, 0)
-        red1[0, i] = acc.astype(BF16).reshape(4, 16, lw)
+    def reduce1(i, more):
+        ls = [lrow[i, x], lr1[0, 0, i], lr1[0, 1, i]] + ([lrd[0]] if more else [])
+        blocks = [pout[i, x], r1[0, 0, i], r1[0, 1, i]] + ([rd[0]] if more else [])
+        ws, ln = weights(ls)
+        red1[0, i] = blend(blocks, ws, 64, 0).astype(BF16).reshape(4, 16, lw)
         lred[0, i] = ln
-        ws, ln = weights([lrow[half + i, z], lr1[1, 0, i], lr1[1, 1, i]])
-        acc = blend([pout[half + i, :, z], r1[1, 0, i], r1[1, 1, i]], ws, 64, 0)
-        red1[1, i] = acc.astype(BF16).reshape(4, 16, lw)
+        r = half + i
+        ls = [lrow[r, z], lr1[1, 0, i], lr1[1, 1, i]] + ([lrd[1]] if more else [])
+        blocks = [pout[r, :, z], r1[1, 0, i], r1[1, 1, i]] + ([rd[1]] if more else [])
+        ws, ln = weights(ls)
+        red1[1, i] = blend(blocks, ws, 64, 0).astype(BF16).reshape(4, 16, lw)
         lred[1, i] = ln
 
     def reduce2(i):
@@ -335,43 +394,74 @@
         def _():
             start(near(t + first))
 
+        @pl.when((t + first < half) & ((t + first) % 2 == 0))
+        def _():
+            start(near_pe((t + first) // 2))
+
         @pl.when(t < half)
         def _():
             near_in(t)
             start(direct(t))
 
-        i1 = t - 1
+        @pl.when((t < half) & (t % 2 == 0))
+        def _():
+            near_pe_in(t // 2)
+            start(direct_pe(t // 2))
+
+        i1 = t - 2
 
         @pl.when((i1 >= 0) & (i1 < half))
         def _():
             relay(i1)
 
-        i2 = t - 2
+        @pl.when((i1 >= 0) & (i1 < half) & (i1 % 2 == 0))
+        def _():
+            relay_pe(i1 // 2)
+
+        i2 = t - 4
+
+        @pl.when((i2 >= 0) & (i2 < half) & (i2 % 2 == 0))
+        def _():
+            onward_pe_in(i2 // 2)
 
         @pl.when((i2 >= 0) & (i2 < half))
         def _():
             onward_in(i2)
             attend(i2, 0)
             attend(half + i2, 1)
+
+        @pl.when((i2 >= 0) & (i2 < last))
+        def _():
             start(far(i2))
 
-        i3 = t - 3
-
-        @pl.when((i3 >= 0) & (i3 < half))
+        @pl.when(i2 == last)
+        def _():
+            start(straight() + scatter1(last))
+
+        i3 = t - 6
+
+        @pl.when((i3 >= 0) & (i3 < last))
         def _():
             far_in(i3)
             middle(i3)
             start(scatter1(i3))
 
-        i5 = t - 5
-
-        @pl.when((i5 >= 0) & (i5 < half))
+        i5 = t - 8
+
+        @pl.when((i5 >= 0) & (i5 < last))
         def _():
             scatter1_in(i5)
-            reduce1(i5)
+            reduce1(i5, False)
             start(scatter2(i5))
 
-        i7 = t - 7
+        @pl.when(i5 == last)
+        def _():
+            scatter1_in(i5)
+            straight_in()
+            reduce1(i5, True)
+            start(scatter2(i5))
+
+        i7 = t - 10
 
         @pl.when(i7 >= 0)
         def _():
@@ -380,7 +470,7 @@
 
         return carry
 
-    lax.fori_loop(0, half + 7, step, 0)
+    lax.fori_loop(0, half + 10, step, 0)
 
     w_copies[1].wait()
     lse = flse[...].reshape(rows, 128)[:, :1]
@@ -397,12 +487,13 @@
         vb0 = jnp.where(hrow == j + 4, dot(latent, w_v[j + 4]), 0.0).astype(BF16)
         back = dot(b0, va0) + dot(b1, vb0)
         tx2[:, :, j * 128 : (j + 1) * 128] = back.astype(BF16).reshape(ngrp, 16, 128)
-
-    home = [
-        rcopy(tx2.at[lax.rem(g + k, ngrp)], rx2.at[g], out_sem.at[10], rb_r.at[0], gid(k))
-        for k in range(1, ngrp)
-    ]
-    start(home)
+        if j % 2 == 1:
+            part = pl.ds((j - 1) * 128, 256)
+            start([
+                rcopy(tx2.at[d, :, part], rx2.at[g, :, part], out_sem.at[10], rb_r.at[0], {"grp": d})
+                for d in dst
+            ])
+
     rx2[g] = tx2[g]
 
     def left(ref, n):
@@ -412,12 +503,16 @@
     left(qall.at[pl.ds(0, 8)], 1)
     left(qall.at[pl.ds(0, 4)], 2)
     left(pout.at[pl.ds(0, 4)], 3)
-    left(lrow.at[pl.ds(0, 8)], 4)
+    left(lrow.at[pl.ds(0, 10), pl.ds(0, 3)], 4)
     left(pout.at[pl.ds(0, 8)], 5)
     left(lrow.at[pl.ds(0, 8)], 6)
     left(pout.at[pl.ds(0, 3)], 7)
     left(lrow.at[pl.ds(0, 12)], 8)
+    left(qpe.at[pl.ds(0, 3), :, pl.ds(0, 2)], 11)
+    left(qpe.at[pl.ds(0, 4)], 12)
+    left(qpe.at[pl.ds(0, 2)], 13)
     all_routed.wait_send()
+    more_routed.wait_send()
     all_home = rcopy(tx2.at[most], rx2.at[most], out_sem.at[10], rb_r.at[0], gid(1))
     all_home.wait_recv()
     got = rx2[...].reshape(bl, lw)
@@ -453,16 +548,21 @@
             pltpu.VMEM((nreq, width, blk), BF16),
             pltpu.VMEM((heads * nope, lw), BF16),
             pltpu.VMEM((heads, lw, 128), BF16),
-            pltpu.VMEM((ngrp, 16, 1088), BF16),
-            pltpu.VMEM((ngrp, 16, 1088), BF16),
+            pltpu.VMEM((ngrp, 16, lw), BF16),
+            pltpu.VMEM((ngrp, 16, lw), BF16),
+            pltpu.VMEM((ngrp, 16, width), BF16),
+            pltpu.VMEM((ngrp, 16, width), BF16),
             pltpu.VMEM((rows, width), BF16),
-            pltpu.VMEM((nreq, NX, NZ, 16, width), BF16),
+            pltpu.VMEM((nreq, NX, NZ, 16, lw), BF16),
+            pltpu.VMEM((half, NX, NZ, 16, 128), BF16),
             pltpu.VMEM((nreq, NX, NZ, 16, lw), BF16),
             pltpu.VMEM((nreq, 4, 1, 128), F32),
             pltpu.VMEM((2, 2, half, 2, 16, lw), BF16),
             pltpu.VMEM((2, 2, half, 1, 128), F32),
             pltpu.VMEM((2, 2, half, 4, 16, lw), BF16),
             pltpu.VMEM((2, 2, half, 1, 128), F32),
+            pltpu.VMEM((2, 4, 16, lw), BF16),
+            pltpu.VMEM((2, 1, 128), F32),
             pltpu.VMEM((2, half, 4, 16, lw), BF16),
             pltpu.VMEM((2, half, 1, 128), F32),
             pltpu.VMEM((2, 3, half, 16, lw), BF16),
@@ -471,8 +571,9 @@
             pltpu.VMEM((nreq, 16, 128), F32),
             pltpu.VMEM((ngrp, 16, lw), BF16),
             pltpu.VMEM((ngrp, 16, lw), BF16),
-            dma((nreq,)), dma((2,)), dma((11,)), dma((1,)), dma((1,)),
+            dma((nreq,)), dma((2,)), dma((15,)), dma((1,)), dma((1,)), dma((1,)),
             dma((half,)), dma((half,)), dma((half,)),
+            dma((half // 2,)), dma((half // 2,)), dma((half // 2,)),
             dma((2, half)), dma((2, half)), dma((2, half)),
         ],
         compiler_params=pltpu.CompilerParams(

time: 85.7 us -> 77.1 us (0.90)
  Pallas kernels: 84 us -> 75.4 us
    pallas_call x1, Pallas kernels: 84 us -> 75.4 us  [on_device(): pl.pallas_call(functools.partial(kernel, ngrp, nreq, blk, scale2), out_sh...]
where the time goes in v1:
time: 77.1 us; the launch traced here: 76.9 us
  Pallas kernels  75.4 us (98%)
  local copies, waits for them, and re-layouts  1.47 us (2%)
    pallas_call x1, Pallas kernels, on_device(): pl.pallas_call(functools.partial(kernel, ngrp, nreq, blk, scale2), out_sh...  75.4 us

profile of v1, /device:TPU:1, one launch (start us, length us, event | category | flops | bytes accessed | tf_op | source)
XLA Modules:
  0.0 76.9 jit_solution(8203201575274120610)
XLA Ops:
  0.0 75.4 %shard_map.82 = bf16[32,1024]{1,0:T(8,128)(2,1)} custom-call(s32[128]{0:T(128)} %lens.1, s32[8,16]{1,0:T(8,128)} %slots.1, bf16[32,1024]{1,0:T(8,128)(2,1)} %bitcast.9, bf16[32,512]{1,0:T(8,128)(2,1)} %bitcast.11, bf16[32,576]{1,0:T(8,128)(2,1)} %bitcast.10, bf16[1024,512]{1,0:T(8,128)(2,1)} %bitcast.8, bf16[8,512,128]{2,1,0:T(8,128)(2,1)} %w_v_hbm.1, ...), custom_call_target="tpu_custom_call" | custom-call | flops 9126805504 | bytes 18874368 | tf_op jit(solution)/shard_map/pallas_call | solution.py:541
  75.4 1.5 %copy.10 = bf16[2,16,1024]{2,1,0:T(8,128)(2,1)} copy(bf16[2,16,1024]{2,1,0:T(8,128)(2,1)} %bitcast.6) | data formatting | bytes 131072

commit v2 on v1

--- a/solution.py
+++ b/solution.py
@@ -37,9 +37,9 @@
     ngrp, nreq, blk, scale2,
     lens, slots, qn, qp, lat, w_uk_hbm, w_v_hbm, cache,
     out,
-    cbuf, w_uk, w_v, tx, rx, ty, ry, latrep, qall, qpe, pout, lrow, h1, lh1, r1, lr1, rd, lrd, red1, lred, r2, lr2,
+    cbuf, w_uk, w_v, tx, rx, ty, ry, latrep, qall, qpe, pout, lrow, h1, lh1, r1, lr1, rd, lrd, red1, lred, h2, lh2, lred2, r2, lr2,
     fin, flse, tx2, rx2,
-    c_sem, w_sem, out_sem, rt_r, ru_r, rb_r, g1_r, g2_r, g3_r, e1_r, e2_r, e3_r, h_r, s1_r, s2_r,
+    c_sem, w_sem, out_sem, rt_r, ru_r, rb_r, g0_r, g1_r, g2_r, g3_r, e1_r, e2_r, e3_r, h_r, s1_r, h2_r, s2_r,
 ):
     g = lax.axis_index("grp")
     s = lax.axis_index("seq")
@@ -151,16 +151,23 @@
     def landed(ref, sem):
         rcopy(ref, ref, out_sem.at[0], sem, xid(1)).wait_recv()
 
-    def near(i):
+    def near(i, hops):
         copies = []
-        for k in (1, 3, 2):
+        for k in hops:
             a, b = qall.at[i, x, z], qall.at[half + i, x, z]
             copies.append(rcopy(a, a, out_sem.at[0], g1_r.at[i], zid(k)))
             copies.append(rcopy(b, b, out_sem.at[0], g1_r.at[i], xid(k)))
         return copies
 
-    def near_in(i):
-        landed(qall.at[i, pl.ds(0, 2), pl.ds(0, 3)], g1_r.at[i])
+    straight_steps = 2
+
+    def pass_on(i):
+        landed(qall.at[i, 0], g1_r.at[i])
+        turn = 2 * (i % 2)
+        a = qall.at[i, x, lax.rem(z + 3 + turn, NZ)]
+        b = qall.at[half + i, lax.rem(x + 3 + turn, NX), z]
+        rcopy(a, a, out_sem.at[0], g0_r.at[i], zid(1 + turn)).start()
+        rcopy(b, b, out_sem.at[0], g0_r.at[i], xid(1 + turn)).start()
 
     def direct(i):
         a = qall.at[i, x]
@@ -221,7 +228,7 @@
 
     first = 4
     for i in range(first):
-        start(near(i))
+        start(near(i, (1, 3, 2) if i < straight_steps else (1, 3)))
 
     more_routed.wait_recv()
     spread = dot(m0, ry[:, :, :lw].reshape(bl, lw))
@@ -293,18 +300,43 @@
         landed(pout.at[i], s1_r.at[0, i])
         landed(lrow.at[i], s1_r.at[1, i])
 
+    def far2(i):
+        turn = 2 * (i % 2)
+        return send(red1.at[0, i, zo], h2.at[0, i], lred.at[0, i], lh2.at[0, i], 15, h2_r, i,
+                    zid(1 + turn)) + send(
+            red1.at[1, i, xo], h2.at[1, i], lred.at[1, i], lh2.at[1, i], 15, h2_r, i,
+            xid(1 + turn))
+
+    def far2_in(i):
+        landed(pout.at[i, 0, pl.ds(0, 2)], h2_r.at[0, i])
+        landed(lrow.at[i, pl.ds(0, 2)], h2_r.at[1, i])
+
     def scatter2(i):
         copies = []
+        for j in range(2):
+            xt, zt = (xr, xl)[j], (zr, zl)[j]
+            copies += send(red1.at[0, i, zt], r2.at[0, j, i], lred2.at[0, i], lr2.at[0, j, i],
+                           7, s2_r, i, zid(1 + 2 * j))
+            copies += send(red1.at[1, i, xt], r2.at[1, j, i], lred2.at[1, i], lr2.at[1, j, i],
+                           7, s2_r, i, xid(1 + 2 * j))
+        return copies
+
+    def scatter2_in(i):
+        landed(pout.at[i, 0], s2_r.at[0, i])
+        landed(lrow.at[i], s2_r.at[1, i])
+
+    def straight2():
+        copies = []
         for k in (1, 3, 2):
-            copies += send(red1.at[0, i, lax.rem(z + k, NZ)], r2.at[0, k - 1, i], lred.at[0, i],
-                           lr2.at[0, k - 1, i], 7, s2_r, i, zid(k))
-            copies += send(red1.at[1, i, lax.rem(x + k, NX)], r2.at[1, k - 1, i], lred.at[1, i],
-                           lr2.at[1, k - 1, i], 7, s2_r, i, xid(k))
+            copies += send(red1.at[0, last, lax.rem(z + k, NZ)], r2.at[0, k - 1, last],
+                           lred.at[0, last], lr2.at[0, k - 1, last], 17, s2_r, last, zid(k))
+            copies += send(red1.at[1, last, lax.rem(x + k, NX)], r2.at[1, k - 1, last],
+                           lred.at[1, last], lr2.at[1, k - 1, last], 17, s2_r, last, xid(k))
         return copies
 
-    def scatter2_in(i):
-        landed(pout.at[i, pl.ds(0, 2), pl.ds(0, 3)], s2_r.at[0, i])
-        landed(lrow.at[pl.ds(0, 2), pl.ds(0, 3)], s2_r.at[1, i])
+    def straight2_in():
+        landed(pout.at[last, pl.ds(0, 2), pl.ds(0, 3)], s2_r.at[0, last])
+        landed(lrow.at[pl.ds(0, 2), pl.ds(0, 3)], s2_r.at[1, last])
 
     def weights(ls):
         top = functools.reduce(jnp.maximum, ls)
@@ -382,26 +414,46 @@
         red1[1, i] = blend(blocks, ws, 64, 0).astype(BF16).reshape(4, 16, lw)
         lred[1, i] = ln
 
-    def reduce2(i):
+    def middle2(i):
+        turn = 2 * (i % 2)
         for part, own in ((0, z), (1, x)):
-            ws, ln = weights([lred[part, i]] + [lr2[part, k, i] for k in range(3)])
-            blocks = [red1[part, i, own]] + [r2[part, k, i] for k in range(3)]
+            to = lax.rem(own + 1 + turn, 4)
+            ws, ln = weights([lred[part, i], lh2[part, i]])
+            acc = blend([red1[part, i, to], h2[part, i]], ws, 16, to * 16)
+            red1[part, i, to] = acc.astype(BF16)
+            lred2[part, i] = jnp.where(lane_1 // 16 == to, ln, lred[part, i])
+
+    def reduce2(i, n):
+        for part, own in ((0, z), (1, x)):
+            ws, ln = weights([lred[part, i]] + [lr2[part, k, i] for k in range(n)])
+            blocks = [red1[part, i, own]] + [r2[part, k, i] for k in range(n)]
             fin[part * half + i] = blend(blocks, ws, 16, own * 16)
             flse[part * half + i] = jnp.broadcast_to(column(ln, 16, own * 16), (16, 128))
 
     def step(t, carry):
         @pl.when(t + first < half)
         def _():
-            start(near(t + first))
+            start(near(t + first, (1, 3)))
 
         @pl.when((t + first < half) & ((t + first) % 2 == 0))
         def _():
             start(near_pe((t + first) // 2))
 
+        @pl.when(t < straight_steps)
+        def _():
+            landed(qall.at[t, pl.ds(0, 2), pl.ds(0, 3)], g1_r.at[t])
+
+        @pl.when((t >= straight_steps) & (t < half))
+        def _():
+            landed(qall.at[t, 0, pl.ds(0, 2)], g0_r.at[t])
+
         @pl.when(t < half)
         def _():
-            near_in(t)
             start(direct(t))
+
+        @pl.when(t + straight_steps < half)
+        def _():
+            pass_on(t + straight_steps)
 
         @pl.when((t < half) & (t % 2 == 0))
         def _():
@@ -452,25 +504,38 @@
         def _():
             scatter1_in(i5)
             reduce1(i5, False)
-            start(scatter2(i5))
+            start(far2(i5))
 
         @pl.when(i5 == last)
         def _():
             scatter1_in(i5)
             straight_in()
             reduce1(i5, True)
-            start(scatter2(i5))
-
-        i7 = t - 10
-
-        @pl.when(i7 >= 0)
+            start(straight2())
+
+        i6 = t - 9
+
+        @pl.when((i6 >= 0) & (i6 < last))
+        def _():
+            far2_in(i6)
+            middle2(i6)
+            start(scatter2(i6))
+
+        i7 = t - 11
+
+        @pl.when((i7 >= 0) & (i7 < last))
         def _():
             scatter2_in(i7)
-            reduce2(i7)
+            reduce2(i7, 2)
+
+        @pl.when(i7 == last)
+        def _():
+            straight2_in()
+            reduce2(last, 3)
 
         return carry
 
-    lax.fori_loop(0, half + 10, step, 0)
+    lax.fori_loop(0, half + 11, step, 0)
 
     w_copies[1].wait()
     lse = flse[...].reshape(rows, 128)[:, :1]
@@ -506,8 +571,12 @@
     left(lrow.at[pl.ds(0, 10), pl.ds(0, 3)], 4)
     left(pout.at[pl.ds(0, 8)], 5)
     left(lrow.at[pl.ds(0, 8)], 6)
-    left(pout.at[pl.ds(0, 3)], 7)
-    left(lrow.at[pl.ds(0, 12)], 8)
+    left(pout.at[pl.ds(0, 7), 0], 7)
+    left(lrow.at[pl.ds(0, 7)], 8)
+    left(pout.at[pl.ds(0, 7), 0, pl.ds(0, 2)], 15)
+    left(lrow.at[pl.ds(0, 7), pl.ds(0, 2)], 16)
+    left(pout.at[0, pl.ds(0, 2), pl.ds(0, 3)], 17)
+    left(lrow.at[pl.ds(0, 2), pl.ds(0, 3)], 18)
     left(qpe.at[pl.ds(0, 3), :, pl.ds(0, 2)], 11)
     left(qpe.at[pl.ds(0, 4)], 12)
     left(qpe.at[pl.ds(0, 2)], 13)
@@ -565,16 +634,19 @@
             pltpu.VMEM((2, 1, 128), F32),
             pltpu.VMEM((2, half, 4, 16, lw), BF16),
             pltpu.VMEM((2, half, 1, 128), F32),
+            pltpu.VMEM((2, half, 16, lw), BF16),
+            pltpu.VMEM((2, half, 1, 128), F32),
+            pltpu.VMEM((2, half, 1, 128), F32),
             pltpu.VMEM((2, 3, half, 16, lw), BF16),
             pltpu.VMEM((2, 3, half, 1, 128), F32),
             pltpu.VMEM((nreq, 16, lw), F32),
             pltpu.VMEM((nreq, 16, 128), F32),
             pltpu.VMEM((ngrp, 16, lw), BF16),
             pltpu.VMEM((ngrp, 16, lw), BF16),
-            dma((nreq,)), dma((2,)), dma((15,)), dma((1,)), dma((1,)), dma((1,)),
-            dma((half,)), dma((half,)), dma((half,)),
+            dma((nreq,)), dma((2,)), dma((19,)), dma((1,)), dma((1,)), dma((1,)),
+            dma((half,)), dma((half,)), dma((half,)), dma((half,)),
             dma((half // 2,)), dma((half // 2,)), dma((half // 2,)),
-            dma((2, half)), dma((2, half)), dma((2, half)),
+            dma((2, half)), dma((2, half)), dma((2, half)), dma((2, half)),
         ],
         compiler_params=pltpu.CompilerParams(
             collective_id=0, has_side_effects=True, vmem_limit_bytes=58 * 1024 * 1024

time: 77.1 us -> 80.8 us (1.048)
  Pallas kernels: 75.4 us -> 79.1 us
    pallas_call x1, Pallas kernels: 75.4 us -> 79.1 us  [on_device(): pl.pallas_call(functools.partial(kernel, ngrp, nreq, blk, scale2), out_sh...]
where the time goes in v2:
time: 80.8 us; the launch traced here: 80.6 us
  Pallas kernels  79.1 us (98%)
  local copies, waits for them, and re-layouts  1.47 us (2%)
    pallas_call x1, Pallas kernels, on_device(): pl.pallas_call(functools.partial(kernel, ngrp, nreq, blk, scale2), out_sh...  79.1 us

profile of v2, /device:TPU:1, one launch (start us, length us, event | category | flops | bytes accessed | tf_op | source)
XLA Modules:
  0.0 80.6 jit_solution(17244471526765261828)
XLA Ops:
  0.0 79.1 %shard_map.82 = bf16[32,1024]{1,0:T(8,128)(2,1)} custom-call(s32[128]{0:T(128)} %lens.1, s32[8,16]{1,0:T(8,128)} %slots.1, bf16[32,1024]{1,0:T(8,128)(2,1)} %bitcast.9, bf16[32,512]{1,0:T(8,128)(2,1)} %bitcast.11, bf16[32,576]{1,0:T(8,128)(2,1)} %bitcast.10, bf16[1024,512]{1,0:T(8,128)(2,1)} %bitcast.8, bf16[8,512,128]{2,1,0:T(8,128)(2,1)} %w_v_hbm.1, ...), custom_call_target="tpu_custom_call" | custom-call | flops 9126805504 | bytes 18874368 | tf_op jit(solution)/shard_map/pallas_call | solution.py:610
  79.1 1.5 %copy.10 = bf16[2,16,1024]{2,1,0:T(8,128)(2,1)} copy(bf16[2,16,1024]{2,1,0:T(8,128)(2,1)} %bitcast.6) | data formatting | bytes 131072

commit v3 on v1

--- a/solution.py
+++ b/solution.py
@@ -39,7 +39,7 @@
     out,
     cbuf, w_uk, w_v, tx, rx, ty, ry, latrep, qall, qpe, pout, lrow, h1, lh1, r1, lr1, rd, lrd, red1, lred, r2, lr2,
     fin, flse, tx2, rx2,
-    c_sem, w_sem, out_sem, rt_r, ru_r, rb_r, g1_r, g2_r, g3_r, e1_r, e2_r, e3_r, h_r, s1_r, s2_r,
+    c_sem, w_sem, out_sem, rt_r, ru_r, rb_r, g0_r, g1_r, g2_r, g3_r, e1_r, e2_r, e3_r, h_r, s1_r, s2_r,
 ):
     g = lax.axis_index("grp")
     s = lax.axis_index("seq")
@@ -151,16 +151,23 @@
     def landed(ref, sem):
         rcopy(ref, ref, out_sem.at[0], sem, xid(1)).wait_recv()
 
-    def near(i):
+    def near(i, hops):
         copies = []
-        for k in (1, 3, 2):
+        for k in hops:
             a, b = qall.at[i, x, z], qall.at[half + i, x, z]
             copies.append(rcopy(a, a, out_sem.at[0], g1_r.at[i], zid(k)))
             copies.append(rcopy(b, b, out_sem.at[0], g1_r.at[i], xid(k)))
         return copies
 
-    def near_in(i):
-        landed(qall.at[i, pl.ds(0, 2), pl.ds(0, 3)], g1_r.at[i])
+    straight_steps = 2
+
+    def pass_on(i):
+        landed(qall.at[i, 0], g1_r.at[i])
+        turn = 2 * (i % 2)
+        a = qall.at[i, x, lax.rem(z + 3 + turn, NZ)]
+        b = qall.at[half + i, lax.rem(x + 3 + turn, NX), z]
+        rcopy(a, a, out_sem.at[0], g0_r.at[i], zid(1 + turn)).start()
+        rcopy(b, b, out_sem.at[0], g0_r.at[i], xid(1 + turn)).start()
 
     def direct(i):
         a = qall.at[i, x]
@@ -221,7 +228,7 @@
 
     first = 4
     for i in range(first):
-        start(near(i))
+        start(near(i, (1, 3, 2) if i < straight_steps else (1, 3)))
 
     more_routed.wait_recv()
     spread = dot(m0, ry[:, :, :lw].reshape(bl, lw))
@@ -392,16 +399,27 @@
     def step(t, carry):
         @pl.when(t + first < half)
         def _():
-            start(near(t + first))
+            start(near(t + first, (1, 3)))
 
         @pl.when((t + first < half) & ((t + first) % 2 == 0))
         def _():
             start(near_pe((t + first) // 2))
 
+        @pl.when(t < straight_steps)
+        def _():
+            landed(qall.at[t, pl.ds(0, 2), pl.ds(0, 3)], g1_r.at[t])
+
+        @pl.when((t >= straight_steps) & (t < half))
+        def _():
+            landed(qall.at[t, 0, pl.ds(0, 2)], g0_r.at[t])
+
         @pl.when(t < half)
         def _():
-            near_in(t)
             start(direct(t))
+
+        @pl.when(t + straight_steps < half)
+        def _():
+            pass_on(t + straight_steps)
 
         @pl.when((t < half) & (t % 2 == 0))
         def _():
@@ -446,7 +464,7 @@
             middle(i3)
             start(scatter1(i3))
 
-        i5 = t - 8
+        i5 = t - 9
 
         @pl.when((i5 >= 0) & (i5 < last))
         def _():
@@ -461,7 +479,7 @@
             reduce1(i5, True)
             start(scatter2(i5))
 
-        i7 = t - 10
+        i7 = t - 12
 
         @pl.when(i7 >= 0)
         def _():
@@ -470,7 +488,7 @@
 
         return carry
 
-    lax.fori_loop(0, half + 10, step, 0)
+    lax.fori_loop(0, half + 12, step, 0)
 
     w_copies[1].wait()
     lse = flse[...].reshape(rows, 128)[:, :1]
@@ -572,7 +590,7 @@
             pltpu.VMEM((ngrp, 16, lw), BF16),
             pltpu.VMEM((ngrp, 16, lw), BF16),
             dma((nreq,)), dma((2,)), dma((15,)), dma((1,)), dma((1,)), dma((1,)),
-            dma((half,)), dma((half,)), dma((half,)),
+            dma((half,)), dma((half,)), dma((half,)), dma((half,)),
             dma((half // 2,)), dma((half // 2,)), dma((half // 2,)),
             dma((2, half)), dma((2, half)), dma((2, half)),
         ],

time: 77.1 us -> 75.8 us (0.983)
  Pallas kernels: 75.4 us -> 74.2 us
    pallas_call x1, Pallas kernels: 75.4 us -> 74.2 us  [on_device(): pl.pallas_call(functools.partial(kernel, ngrp, nreq, blk, scale2), out_sh...]
where the time goes in v3:
time: 75.8 us; the launch traced here: 75.6 us
  Pallas kernels  74.2 us (98%)
  local copies, waits for them, and re-layouts  1.47 us (2%)
    pallas_call x1, Pallas kernels, on_device(): pl.pallas_call(functools.partial(kernel, ngrp, nreq, blk, scale2), out_sh...  74.2 us

profile of v3, /device:TPU:1, one launch (start us, length us, event | category | flops | bytes accessed | tf_op | source)
XLA Modules:
  0.0 75.6 jit_solution(2042912716355343768)
XLA Ops:
  0.0 74.2 %shard_map.82 = bf16[32,1024]{1,0:T(8,128)(2,1)} custom-call(s32[128]{0:T(128)} %lens.1, s32[8,16]{1,0:T(8,128)} %slots.1, bf16[32,1024]{1,0:T(8,128)(2,1)} %bitcast.9, bf16[32,512]{1,0:T(8,128)(2,1)} %bitcast.11, bf16[32,576]{1,0:T(8,128)(2,1)} %bitcast.10, bf16[1024,512]{1,0:T(8,128)(2,1)} %bitcast.8, bf16[8,512,128]{2,1,0:T(8,128)(2,1)} %w_v_hbm.1, ...), custom_call_target="tpu_custom_call" | custom-call | flops 9126805504 | bytes 18874368 | tf_op jit(solution)/shard_map/pallas_call | solution.py:559
  74.2 1.5 %copy.10 = bf16[2,16,1024]{2,1,0:T(8,128)(2,1)} copy(bf16[2,16,1024]{2,1,0:T(8,128)(2,1)} %bitcast.6) | data formatting | bytes 131072

commit v4 on v3

--- a/solution.py
+++ b/solution.py
@@ -38,7 +38,7 @@
     lens, slots, qn, qp, lat, w_uk_hbm, w_v_hbm, cache,
     out,
     cbuf, w_uk, w_v, tx, rx, ty, ry, latrep, qall, qpe, pout, lrow, h1, lh1, r1, lr1, rd, lrd, red1, lred, r2, lr2,
-    fin, flse, tx2, rx2,
+    fin, flse, early, tx2, rx2,
     c_sem, w_sem, out_sem, rt_r, ru_r, rb_r, g0_r, g1_r, g2_r, g3_r, e1_r, e2_r, e3_r, h_r, s1_r, s2_r,
 ):
     g = lax.axis_index("grp")
@@ -122,13 +122,19 @@
     most = pl.ds(0, ngrp - 1)
     all_routed = rcopy(tx.at[most], rx.at[most], out_sem.at[9], rt_r.at[0], gid(1))
     more_routed = rcopy(ty.at[most], ry.at[most], out_sem.at[14], ru_r.at[0], gid(1))
-    all_routed.wait_recv()
-
     col_l = iota((rows, bl), 1)
     pulls = [jnp.where(col_l == sig + 2 * CAP * f, 1.0, 0.0) for f in range(2)]
     m0, m1 = [v.astype(BF16) for v in pulls]
     own = iota((rows, lw), 0) % 8
     lane = iota((rows, lw), 1)
+    def part_of(v, h):
+        n = rows // 4
+        return jnp.concatenate([v[n * h : n * h + n], v[n * h + 2 * n : n * h + 3 * n]], axis=0)
+
+    backs = [[part_of(v, h).T.astype(BF16) for v in pulls] for h in range(2)]
+    keeps = [[sends[f][t].T.astype(BF16) for t in range(2)] for f in range(2)]
+    all_routed.wait_recv()
+
     w_copies[0].wait()
     absorbed = jnp.zeros((rows, lw), F32)
     for j in range(2):
@@ -396,6 +402,28 @@
             fin[part * half + i] = blend(blocks, ws, 16, own * 16)
             flse[part * half + i] = jnp.broadcast_to(column(ln, 16, own * 16), (16, 128))
 
+    def latents(h):
+        n = rows // 4
+        r = half // 2
+        one, other = pl.ds(r * h, r), pl.ds(half + r * h, r)
+        lse = jnp.concatenate([flse[one].reshape(n, 128), flse[other].reshape(n, 128)], axis=0)
+        own_num = jnp.concatenate([fin[one].reshape(n, lw), fin[other].reshape(n, lw)], axis=0)
+        lse = lse[:, :1]
+        high = part_of(ftop, h)
+        top = jnp.maximum(high, lse)
+        wc = jnp.exp2(lse - top)
+        wn = jnp.exp2(high - top)
+        den = wc + wn * part_of(fden, h)
+        num = wc * own_num + wn * part_of(fnum, h)
+        return (num * (1.0 / den)).astype(BF16)
+
+    hrow = iota((rows // 2, 128), 0) % 8
+
+    def project(latent, h, j):
+        low = jnp.where(hrow == j, dot(latent, w_v[j]), 0.0).astype(BF16)
+        high = jnp.where(hrow == j + 4, dot(latent, w_v[j + 4]), 0.0).astype(BF16)
+        return dot(backs[h][0], low) + dot(backs[h][1], high)
+
     def step(t, carry):
         @pl.when(t + first < half)
         def _():
@@ -486,32 +514,28 @@
             scatter2_in(i7)
             reduce2(i7)
 
+        @pl.when(i7 == half // 2 - 1)
+        def _():
+            w_copies[1].wait()
+            latent = latents(0)
+            for j in range(4):
+                early[:, j * 128 : (j + 1) * 128] = project(latent, 0, j)
+
         return carry
 
     lax.fori_loop(0, half + 12, step, 0)
 
-    w_copies[1].wait()
-    lse = flse[...].reshape(rows, 128)[:, :1]
-    top = jnp.maximum(ftop, lse)
-    wc = jnp.exp2(lse - top)
-    wn = jnp.exp2(ftop - top)
-    den = wc + wn * fden
-    num = wc * fin[...].reshape(rows, lw) + wn * fnum
-    latent = (num * (1.0 / den)).astype(BF16)
-    b0, b1 = [v.T.astype(BF16) for v in pulls]
-    hrow = iota((rows, 128), 0) % 8
+    latent = latents(1)
     for j in range(4):
-        va0 = jnp.where(hrow == j, dot(latent, w_v[j]), 0.0).astype(BF16)
-        vb0 = jnp.where(hrow == j + 4, dot(latent, w_v[j + 4]), 0.0).astype(BF16)
-        back = dot(b0, va0) + dot(b1, vb0)
-        tx2[:, :, j * 128 : (j + 1) * 128] = back.astype(BF16).reshape(ngrp, 16, 128)
+        cols = pl.ds(j * 128, 128)
+        back = early[:, cols] + project(latent, 1, j)
+        tx2[:, :, cols] = back.astype(BF16).reshape(ngrp, 16, 128)
         if j % 2 == 1:
             part = pl.ds((j - 1) * 128, 256)
             start([
                 rcopy(tx2.at[d, :, part], rx2.at[g, :, part], out_sem.at[10], rb_r.at[0], {"grp": d})
                 for d in dst
             ])
-
     rx2[g] = tx2[g]
 
     def left(ref, n):
@@ -536,7 +560,7 @@
     got = rx2[...].reshape(bl, lw)
     for f in range(2):
         for t in range(2):
-            kept = dot(sends[f][t].T.astype(BF16), got)
+            kept = dot(keeps[f][t], got)
             out[pl.ds(t * nreq, nreq), pl.ds(f * lw, lw)] = kept.astype(BF16)
 
     all_home.wait_send()
@@ -587,6 +611,7 @@
             pltpu.VMEM((2, 3, half, 1, 128), F32),
             pltpu.VMEM((nreq, 16, lw), F32),
             pltpu.VMEM((nreq, 16, 128), F32),
+            pltpu.VMEM((16 * ngrp, lw), F32),
             pltpu.VMEM((ngrp, 16, lw), BF16),
             pltpu.VMEM((ngrp, 16, lw), BF16),
             dma((nreq,)), dma((2,)), dma((15,)), dma((1,)), dma((1,)), dma((1,)),

time: 75.8 us -> 76.6 us (1.011)
  no operation moved by 1% of the time
where the time goes in v4:
time: 76.6 us; the launch traced here: 76.4 us
  Pallas kernels  74.9 us (98%)
  local copies, waits for them, and re-layouts  1.47 us (2%)
    pallas_call x1, Pallas kernels, on_device(): pl.pallas_call(functools.partial(kernel, ngrp, nreq, blk, scale2), out_sh...  74.9 us

profile of v4, /device:TPU:1, one launch (start us, length us, event | category | flops | bytes accessed | tf_op | source)
XLA Modules:
  0.0 76.4 jit_solution(12779866133362741561)
XLA Ops:
  0.0 74.9 %shard_map.82 = bf16[32,1024]{1,0:T(8,128)(2,1)} custom-call(s32[128]{0:T(128)} %lens.1, s32[8,16]{1,0:T(8,128)} %slots.1, bf16[32,1024]{1,0:T(8,128)(2,1)} %bitcast.9, bf16[32,512]{1,0:T(8,128)(2,1)} %bitcast.11, bf16[32,576]{1,0:T(8,128)(2,1)} %bitcast.10, bf16[1024,512]{1,0:T(8,128)(2,1)} %bitcast.8, bf16[8,512,128]{2,1,0:T(8,128)(2,1)} %w_v_hbm.1, ...), custom_call_target="tpu_custom_call" | custom-call | flops 9126805504 | bytes 18874368 | tf_op jit(solution)/shard_map/pallas_call | solution.py:583
  74.9 1.5 %copy.10 = bf16[2,16,1024]{2,1,0:T(8,128)(2,1)} copy(bf16[2,16,1024]{2,1,0:T(8,128)(2,1)} %bitcast.6) | data formatting | bytes 131072

commit v5 on v3

--- a/solution.py
+++ b/solution.py
@@ -396,6 +396,9 @@
             fin[part * half + i] = blend(blocks, ws, 16, own * 16)
             flse[part * half + i] = jnp.broadcast_to(column(ln, 16, own * 16), (16, 128))
 
+    def of_part(copies, part):
+        return [c for n, c in enumerate(copies) if n // 2 % 2 == part]
+
     def step(t, carry):
         @pl.when(t + first < half)
         def _():
@@ -445,16 +448,16 @@
         @pl.when((i2 >= 0) & (i2 < half))
         def _():
             onward_in(i2)
-            attend(i2, 0)
-            attend(half + i2, 1)
-
-        @pl.when((i2 >= 0) & (i2 < last))
-        def _():
-            start(far(i2))
-
-        @pl.when(i2 == last)
-        def _():
-            start(straight() + scatter1(last))
+            for part in range(2):
+                attend(part * half + i2, part)
+
+                @pl.when(i2 < last)
+                def _():
+                    start(of_part(far(i2), part))
+
+                @pl.when(i2 == last)
+                def _():
+                    start(of_part(straight() + scatter1(last), part))
 
         i3 = t - 6
 

time: 75.8 us -> 75.8 us (level)
  no operation moved by 1% of the time
where the time goes in v5:
time: 75.8 us; the launch traced here: 75.6 us
  Pallas kernels  74.1 us (98%)
  local copies, waits for them, and re-layouts  1.47 us (2%)
    pallas_call x1, Pallas kernels, on_device(): pl.pallas_call(functools.partial(kernel, ngrp, nreq, blk, scale2), out_sh...  74.1 us

profile of v5, /device:TPU:1, one launch (start us, length us, event | category | flops | bytes accessed | tf_op | source)
XLA Modules:
  0.0 75.6 jit_solution(7134096675018935446)
XLA Ops:
  0.0 74.1 %shard_map.82 = bf16[32,1024]{1,0:T(8,128)(2,1)} custom-call(s32[128]{0:T(128)} %lens.1, s32[8,16]{1,0:T(8,128)} %slots.1, bf16[32,1024]{1,0:T(8,128)(2,1)} %bitcast.9, bf16[32,512]{1,0:T(8,128)(2,1)} %bitcast.11, bf16[32,576]{1,0:T(8,128)(2,1)} %bitcast.10, bf16[1024,512]{1,0:T(8,128)(2,1)} %bitcast.8, bf16[8,512,128]{2,1,0:T(8,128)(2,1)} %w_v_hbm.1, ...), custom_call_target="tpu_custom_call" | custom-call | flops 9126805504 | bytes 18874368 | tf_op jit(solution)/shard_map/pallas_call | solution.py:562
  74.1 1.5 %copy.10 = bf16[2,16,1024]{2,1,0:T(8,128)(2,1)} copy(bf16[2,16,1024]{2,1,0:T(8,128)(2,1)} %bitcast.6) | data formatting | bytes 131072
